TPU v7x, 32 devices: a whole 2x2x4 slice. The times are simulated.
32 devices in a mesh: groups: 2 (over y), slab: 16 (over z, x, core).
Axes of the slice: x: 2, y: 2, z: 4, core: 2. Of those that a mesh axis runs over, the one named last changes fastest.
Arguments:
- volume: bfloat16 [4096, 32, 2048], P(('groups', 'slab')), parts along dimension 0, may hold values from 0 to 2
- measured: bfloat16 [32, 512, 2048], P(('groups', 'slab')), parts along dimension 0, may hold values from 0 to 80
- path_weights: bfloat16 [16, 32], replicated, may hold values from 0.25 to 1
- fractions: float32 [16, 2048], replicated, may hold values from 0.1 to 0.5
- bases: int32 [16], replicated, may hold values from 1 to 1536, as said below
Outputs:
- new_volume: float32 [4096, 32, 2048], P(('groups', 'slab')), parts along dimension 0
There are 2 independent parts, one for each index of `groups`. A program takes and returns all parts, laid end to end along the dimension named above; an argument that names none is the same for every part. Nothing has to cross between parts.
Inputs may be any that keep to these rules, and one draw needn't show every extreme that they name: `bases`: the entries, taken in increasing order, begin with 1 and end with 1536, and consecutive ones differ by less than 512; every slice lies within, or directly before, the rows of some projection. The order of the projections along the subset is not that of the helix.
All inputs are finite; a program needn't handle non-finite values.
Results may differ from a plain program's by a relative error of at most 0.002.
Values may be sent and summed in bfloat16 or wider, within the bound.
No kernel may reach another device: no remote copies, remote signals or barrier semaphores. Data moves between devices by JAX's collectives and lax.ppermute only.
A program may use at most 192 MiB of HBM per device.

v0:
```python
import jax
import jax.numpy as jnp
from jax import lax
from jax.sharding import PartitionSpec as P

RELAX = 1.0


def on_device(volume, measured, path_weights, fractions, bases):
    slices = volume.shape[0]
    cols = volume.shape[2]
    local = measured.shape[0]
    rows = measured.shape[1]
    nslab = lax.axis_size("slab")
    device = lax.axis_index("slab")
    first = device * slices
    image = jnp.einsum("ad,zdc->azc", path_weights, volume, preferred_element_type=jnp.float32)
    share_own = lax.dynamic_slice_in_dim(fractions, first, slices, 1)
    offsets = first - bases
    row_now = offsets[:, None] + jnp.arange(slices, dtype=jnp.int32)[None, :]
    valid_now = (row_now >= 0) & (row_now < rows)
    valid_next = (row_now + 1 >= 0) & (row_now + 1 < rows)
    w_now = jnp.where(valid_now, 1.0 - share_own, 0.0)
    w_next = jnp.where(valid_next, share_own, 0.0)
    ray_total = jnp.sum(path_weights.astype(jnp.float32), axis=1)
    my_bases = lax.dynamic_slice_in_dim(bases, device * local, local, 0)
    margin = slices + 1
    lower = jnp.pad((1.0 - share_own)[:, :, None] * image, ((0, 0), (0, 1), (0, 0)))
    upper = jnp.pad(share_own[:, :, None] * image, ((0, 0), (1, 0), (0, 0)))
    slot_rows = offsets[:, None] + jnp.arange(margin, dtype=jnp.int32)[None, :]
    inside = (slot_rows >= 0) & (slot_rows < rows)
    slots = jnp.where(inside[:, :, None], lower + upper, 0.0)
    my_shares = lax.dynamic_slice_in_dim(fractions, device * local, local, 0)
    my_totals = lax.dynamic_slice_in_dim(ray_total, device * local, local, 0)

    def finish(buffer, base, share_row, total, seen):
        forward = buffer[margin : margin + rows]
        window = lax.dynamic_slice_in_dim(share_row, base - 1, rows + 1, 0)
        ray_norm = total * (1.0 - window[1:] + window[:-1])
        resid = ((seen.astype(jnp.float32) - forward) / ray_norm[:, None]).astype(jnp.bfloat16)
        return jnp.pad(resid, ((margin, margin), (0, 0)))

    received = lax.all_to_all(slots, "slab", split_axis=0, concat_axis=0, tiled=True)
    received = received.reshape(nslab, local, margin, cols).transpose(1, 0, 2, 3)

    def settle(parts, base, share_row, total, seen):
        buffer = jnp.zeros((rows + 2 * margin, cols), jnp.float32)

        def accumulate(source, acc):
            start = source * slices - base + margin
            current = lax.dynamic_slice_in_dim(acc, start, margin, 0)
            return lax.dynamic_update_slice_in_dim(acc, current + parts[source], start, 0)

        buffer = lax.fori_loop(0, nslab, accumulate, buffer)
        padded = finish(buffer, base, share_row, total, seen)
        starts = jnp.arange(nslab, dtype=jnp.int32) * slices - base + margin
        return jax.vmap(lambda start: lax.dynamic_slice_in_dim(padded, start, margin, 0))(starts)

    outgoing = jax.vmap(settle)(received, my_bases, my_shares, my_totals, measured)
    outgoing = outgoing.transpose(1, 0, 2, 3).reshape(nslab * local, margin, cols)
    returned = lax.all_to_all(outgoing, "slab", split_axis=0, concat_axis=0, tiled=True)
    resid_now = returned[:, :slices]
    resid_next = returned[:, 1:]
    blend = (
        w_now[:, :, None] * resid_now.astype(jnp.float32)
        + w_next[:, :, None] * resid_next.astype(jnp.float32)
    ).astype(jnp.bfloat16)
    spread = jnp.einsum("ad,azc->zdc", path_weights, blend, preferred_element_type=jnp.float32)
    column_norm = jnp.einsum(
        "ad,az->zd",
        path_weights.astype(jnp.float32),
        w_now + w_next,
        precision=lax.Precision.HIGHEST,
    )
    return volume.astype(jnp.float32) + RELAX * spread / column_norm[:, :, None]


def solution(mesh):
    placed = (P(("groups", "slab"), None, None), P(("groups", "slab"), None, None), P(), P(), P())
    return jax.shard_map(
        on_device,
        mesh=mesh,
        in_specs=placed,
        out_specs=P(("groups", "slab"), None, None),
        check_vma=False,
    )
```

profile of v0, /device:TPU:15, one launch (start us, length us, event | category | flops | bytes accessed | tf_op | source)
XLA Modules:
  0.0 907.9 jit_solution(6111800820717010111)
XLA Ops:
  1.8 15.8 %broadcast_multiply_fusion.1 = (f32[16,128,2048]{2,0,1:T(8,128)}, f32[16,128,2048]{2,0,1:T(8,128)}) fusion(f32[16,128]{0,1:T(8,128)S(1)} %copy.17, f32[16,128]{0,1:T(8,128)S(1)} %copy.18, bf16[128,32,2048]{2,1,0:T(8,128)(2,1)} %param.9, bf16[16,32]{1,0:T(8,128)(2,1)} %param.11), kind=kOutput, calls=%fused_computation.12 | convolution fusion | flops 276824064 | bytes 50349056 | tf_op jit(solution)/shard_map/ad,zdc->azc/dot_general | solution.py:17
  17.6 11.5 %add_select_fusion = f32[16,129,2048]{2,0,1:T(8,128)S(1)} fusion(f32[16,128,2048]{2,0,1:T(8,128)} %get-tuple-element.204, f32[16,128,2048]{2,0,1:T(8,128)} %get-tuple-element.203, pred[16,129]{0,1:T(8,128)(4,1)S(1)} %copy.16), kind=kLoop, calls=%fused_computation.8 | loop fusion | flops 8454144 | bytes 50464784 | tf_op jit(solution)/shard_map/jit(_where)/select_n | solution.py:32
  29.1 19.8 %copy.19 = f32[16,129,2048]{2,1,0:T(8,128)} copy(f32[16,129,2048]{2,0,1:T(8,128)S(1)} %add_select_fusion) | data formatting | bytes 33816576 | tf_op jit(solution)/shard_map/jit(_where)/select_n | solution.py:32
  48.9 6.7 all-to-all-start
  60.4 379.7 %all-to-all-done = f32[16,129,2048]{2,1,0:T(8,128)} async-done(((f32[16,129,2048]{2,1,0:T(8,128)}), f32[16,129,2048]{2,1,0:T(8,128)}, u32[]{:S(2)}, u32[]{:S(2)}) %all-to-all-start) | async-done | bytes 16908320 | tf_op jit(solution)/shard_map/all_to_all | solution.py:43
  443.7 188.7 %while.20 = (s32[]{:T(128)}, f32[1,770,2048]{2,1,0:T(8,128)}, s32[1]{0:T(128)}, f32[1,16,129,2048]{3,2,1,0:T(8,128)}, s32[]{:T(128)}, /*index=5*/s32[]{:T(128)},...) while((s32[]{:T(128)}, f32[1,770,2048]{2,1,0:T(8,128)}, ...), condition=%wide.region_2.3_spmd, body=%wide.region_0.0_spmd.sunk | while | flops 528413 | bytes 6340901 | solution.py:54
  450.8 4.7 scatter.6
  459.0 3.7 fusion.26
  462.7 4.7 scatter.6
  470.8 3.6 fusion.26
  474.5 4.7 scatter.6
  486.3 4.7 scatter.6
  498.0 4.7 scatter.6
  506.2 3.6 fusion.26
  509.8 4.7 scatter.6
  521.6 4.7 scatter.6
  529.7 3.7 fusion.26
  533.5 4.7 scatter.6
  545.3 4.7 scatter.6
  557.1 4.7 scatter.6
  568.8 4.5 scatter.6
  580.4 4.7 scatter.6
  592.1 4.7 scatter.6
  600.3 3.7 fusion.26
  604.0 4.7 scatter.6
  615.8 4.7 scatter.6
  627.6 4.7 scatter.6
  636.1 35.2 %while.21 = (s32[]{:T(128)}, bf16[1,770,2048]{2,1,0:T(8,128)(2,1)S(1)}, s32[16,3]{0,1:T(4,128)S(1)}, bf16[16,129,2048]{2,1,0:T(8,128)(2,1)}, s32[]{:T(128)}) while((s32[]{:T(128)}, bf16[1,770,2048]{2,1,0:T(8,128)(2,1)S(1)}, s32[16,3]{0,1:T(4,128)S(1)}, bf16[16,129,2048]{2,1,0:T(8,128)(2,1)}, s32[]{:T(128)}) %tuple.80), condition=%wide.while_cond.4, body=%wide.while_body.4.sunk | while | flops 2 | bytes 1086561 | solution.py:57
  671.4 4.8 all-to-all-start.1
  676.5 192.4 %all-to-all-done.1 = bf16[16,129,2048]{2,1,0:T(8,128)(2,1)} async-done(((bf16[16,129,2048]{2,1,0:T(8,128)(2,1)}), bf16[16,129,2048]{2,1,0:T(8,128)(2,1)}, u32[]{:S(2)}, u32[]{:S(2)}) %all-to-all-start.1) | async-done | bytes 8454176 | tf_op jit(solution)/shard_map/all_to_all | solution.py:61
  868.9 8.5 add_convert_fusion
  877.4 30.5 %bitcast_add_fusion.1 = f32[128,32,2048]{2,1,0:T(8,128)} fusion(bf16[128,32,2048]{2,1,0:T(8,128)(2,1)} %param.9, f32[128,32]{1,0:T(8,128)S(1)} %fusion.5, bf16[16,128,2048]{2,1,0:T(8,128)(2,1)S(1)} %add_convert_fusion, bf16[16,32]{1,0:T(8,128)(2,1)S(1)} %copy-done.1), kind=kOutput, calls=%fused_computation.7 | convolution fusion | flops 293601280 | bytes 58737664 | tf_op jit(solution)/shard_map/ad,azc->zdc/dot_general | solution.py:68
  (151 shorter events, 132.4 us)
Async XLA Ops:
  48.9 6.7 copy-start.4
  48.9 8.6 copy-start.1
  48.9 394.8 %copy-start.2 = (s32[3]{0:T(128)S(1)}, s32[3]{0:T(128)}, u32[]{:S(2)}) copy-start(s32[3]{0:T(128)} %constant.172.clone.1) | copy-start | bytes 40
  48.9 394.8 %copy-start.3 = (s32[1,2]{1,0:T(1,128)S(1)}, s32[1,2]{1,0:T(1,128)}, u32[]{:S(2)}) copy-start(s32[1,2]{1,0:T(1,128)} %constant.171.clone.1) | copy-start | bytes 28
  48.9 391.3 %all-to-all-start = ((f32[16,129,2048]{2,1,0:T(8,128)}), f32[16,129,2048]{2,1,0:T(8,128)}, u32[]{:S(2)}, u32[]{:S(2)}) async-start(f32[16,129,2048]{2,1,0:T(8,128)} %copy.19), calls=%async_computation | async-start | bytes 35651584 | tf_op jit(solution)/shard_map/all_to_all | solution.py:43
  443.7 188.7 %copy-start = (bf16[1,512,2048]{2,1,0:T(8,128)(2,1)S(1)}, bf16[1,512,2048]{2,1,0:T(8,128)(2,1)}, u32[]{:S(2)}) copy-start(bf16[1,512,2048]{2,1,0:T(8,128)(2,1)} %param.10) | copy-start | bytes 6291460
  671.4 197.6 %all-to-all-start.1 = ((bf16[16,129,2048]{2,1,0:T(8,128)(2,1)}), bf16[16,129,2048]{2,1,0:T(8,128)(2,1)}, u32[]{:S(2)}, u32[]{:S(2)}) async-start(bf16[16,129,2048]{2,1,0:T(8,128)(2,1)} %get-tuple-element.169), calls=%async_computation.1 | async-start | bytes 17825792 | tf_op jit(solution)/shard_map/all_to_all | solution.py:61
where the time goes:
time: 912 us; the launch traced here: 908 us
  waiting for transfers between devices  572 us (63%)
  local copies, waits for them, and re-layouts  147 us (16%)
  other arithmetic  119 us (13%)
  matrix products  46.5 us (5%)
  starting transfers between devices  11.5 us (1%)
  loops' own time  10.3 us (1%)
    all_to_all x1, waiting for transfers between devices, on_device(): lax.all_to_all(slots, 'slab', split_axis=0, concat_axis=0, tiled=True)  380 us
    all_to_all x1, waiting for transfers between devices, on_device(): lax.all_to_all(outgoing, 'slab', split_axis=0, concat_axis=0, tiled=True)  192 us
    another operation x32, other arithmetic  90.9 us
    scatter x16, local copies, waits for them, and re-layouts, accumulate(): lax.dynamic_update_slice_in_dim(acc, current + parts[source], start, 0)  75.7 us
    gather x48, local copies, waits for them, and re-layouts  35.2 us
    dot_general x1, matrix products, on_device(): jnp.einsum('ad,azc->zdc', path_weights, blend, preferred_element_type=jnp...  30.5 us
    select_n x1, local copies, waits for them, and re-layouts, on_device(): slots = jnp.where(inside[:, :, None], lower + upper, 0.0)  19.8 us
  transfers between devices with their start and end apart: 2, of which 2 were waited for; matrix products, arithmetic and copies ran while one was open for 0% of the time, Pallas kernels for 0%

commit v1 on v0

v1 whole, which is shorter than its diff:
```python
import jax
import jax.numpy as jnp
from jax import lax
from jax.experimental import pallas as pl
from jax.experimental.pallas import tpu as pltpu
from jax.sharding import PartitionSpec as P

RELAX = 1.0
BLOCK = 16
HALF = 8
LANES = 128
WIDE = 256


def update_kernel(
    vol_ref, next_ref, left_ref, right_ref, seen_ref, edge_ref, now_ref, prev_ref, inv_ref,
    edge_now_ref, edge_prev_ref, edge_inv_ref, image_w_ref, weight_ref, spread_ref, carry_w_ref,
    out_ref, carry_ref, slab_ref,
):
    block = pl.program_id(1)
    last = pl.num_programs(1) - 1
    depth, width = vol_ref.shape[1:]
    angles = weight_ref.shape[0]
    slab_ref[0 : BLOCK * depth] = vol_ref[...].reshape(BLOCK * depth, width)

    @pl.when(block < last)
    def _():
        slab_ref[BLOCK * depth :] = next_ref[0]

    @pl.when(block == last)
    def _():
        slab_ref[BLOCK * depth :] = right_ref[0]

    def wide(coef):
        return jnp.concatenate([coef] * (WIDE // LANES), axis=1)

    def dot(a, b):
        return jnp.dot(a, b, preferred_element_type=jnp.float32)

    @pl.loop(0, width // WIDE)
    def _(chunk):
        at = pl.ds(pl.multiple_of(chunk * WIDE, WIDE), WIDE)

        @pl.when(block == 0)
        def _():
            weights = weight_ref[...]
            mine = dot(weights, slab_ref[0:depth, at])
            before = dot(weights, left_ref[0, :, at])
            carry_ref[:, at] = (
                edge_ref[:, at].astype(jnp.float32) * wide(edge_inv_ref[...])
                - mine * wide(edge_now_ref[...])
                - before * wide(edge_prev_ref[...])
            ).astype(jnp.bfloat16)

        seen = seen_ref[:, :, at].astype(jnp.float32)
        parts = []
        for half in range(BLOCK // HALF):
            start = half * HALF * depth
            prev = dot(image_w_ref[...], slab_ref[start : start + HALF * depth, at])
            now = dot(image_w_ref[...], slab_ref[start + depth : start + (HALF + 1) * depth, at])
            got = seen[:, half * HALF : (half + 1) * HALF].reshape(angles * HALF, WIDE)
            resid = got * wide(inv_ref[0, half]) - now * wide(now_ref[0, half]) - prev * wide(prev_ref[0, half])
            parts.append(resid.reshape(angles, HALF, WIDE))
        resid = jnp.concatenate(parts, axis=1)
        spread = dot(spread_ref[0], resid.astype(jnp.bfloat16).reshape(angles * BLOCK, WIDE))
        extra = dot(carry_w_ref[0], carry_ref[:, at])
        carry_ref[:, at] = resid[:, BLOCK - 1].astype(jnp.bfloat16)
        volume = slab_ref[0 : BLOCK * depth, at].astype(jnp.float32)
        result = volume + spread
        out_ref[0, :, at] = result[:depth] + extra
        out_ref[1:, :, at] = result[depth:].reshape(BLOCK - 1, depth, WIDE)


def update(volume, left, right, seen, edge, coefs, edge_coefs, image_w, weights, spread_w, carry_w):
    slices, depth, cols = volume.shape
    angles = weights.shape[0]
    blocks = slices // BLOCK
    width = 1024 if angles <= 16 else WIDE
    half_spec = pl.BlockSpec((1, BLOCK // HALF, angles * HALF, LANES), lambda c, b: (b, 0, 0, 0))
    whole2 = lambda shape: pl.BlockSpec(shape, lambda c, b: (0,) * len(shape))
    return pl.pallas_call(
        update_kernel,
        grid=(cols // width, blocks),
        in_specs=[
            pl.BlockSpec((BLOCK, depth, width), lambda c, b: (b, 0, c)),
            pl.BlockSpec((1, depth, width), lambda c, b: (jnp.minimum((b + 1) * BLOCK, slices - 1), 0, c)),
            pl.BlockSpec((1, depth, width), lambda c, b: (0, 0, c)),
            pl.BlockSpec((1, depth, width), lambda c, b: (0, 0, c)),
            pl.BlockSpec((angles, BLOCK, width), lambda c, b: (0, b, c)),
            pl.BlockSpec((angles, width), lambda c, b: (0, c)),
            half_spec, half_spec, half_spec,
            whole2((angles, LANES)), whole2((angles, LANES)), whole2((angles, LANES)),
            whole2(image_w.shape), whole2(weights.shape),
            pl.BlockSpec((1,) + spread_w.shape[1:], lambda c, b: (b, 0, 0)),
            pl.BlockSpec((1,) + carry_w.shape[1:], lambda c, b: (b, 0, 0)),
        ],
        out_specs=pl.BlockSpec((BLOCK, depth, width), lambda c, b: (b, 0, c)),
        out_shape=jax.ShapeDtypeStruct(volume.shape, jnp.float32),
        scratch_shapes=[
            pltpu.VMEM((angles, width), jnp.bfloat16),
            pltpu.VMEM(((BLOCK + 1) * depth, width), jnp.bfloat16),
        ],
        compiler_params=pltpu.CompilerParams(
            dimension_semantics=("arbitrary", "arbitrary"), vmem_limit_bytes=48 * 2**20
        ),
        cost_estimate=pl.CostEstimate(
            flops=4 * slices * depth * cols * angles, bytes_accessed=volume.size * 6 + seen.size * 2, transcendentals=0
        ),
        name="slab_update",
    )(volume, volume, left, right, seen, edge, *coefs, *edge_coefs, image_w, weights, spread_w, carry_w)


def on_device(volume, measured, path_weights, fractions, bases):
    slices, depth, cols = volume.shape
    local, rows = measured.shape[:2]
    nslab = lax.axis_size("slab")
    device = lax.axis_index("slab")
    angles = local * nslab
    first = device * slices
    classes = rows // slices
    planes = nslab // classes
    blocks = slices // BLOCK

    my_bases = lax.dynamic_slice_in_dim(bases, device * local, local, 0)
    turned = jax.vmap(lambda m, b: jnp.roll(m, b - 1, axis=0))(measured, my_bases)
    by_class = turned.reshape(local, classes, slices, cols).transpose(1, 0, 2, 3)
    outgoing = jnp.tile(by_class, (planes, 1, 1, 1)).reshape(nslab * local, slices, cols)
    seen = lax.all_to_all(outgoing, "slab", split_axis=0, concat_axis=0, tiled=True)
    ends = jnp.roll(by_class[:, :, slices - 1], 1, axis=0)
    ends = jnp.tile(ends, (planes, 1, 1)).reshape(nslab * local, cols // LANES, LANES)
    edge = lax.all_to_all(ends, "slab", split_axis=0, concat_axis=0, tiled=True).reshape(angles, cols)
    left = lax.ppermute(volume[slices - 1 :], "slab", [(i, i + 1) for i in range(nslab - 1)])
    right = lax.ppermute(volume[:1], "slab", [(i + 1, i) for i in range(nslab - 1)])

    weights = path_weights.astype(jnp.float32)
    ray_total = jnp.sum(weights, axis=1)[:, None]
    share = lax.dynamic_slice_in_dim(jnp.pad(fractions, ((0, 0), (1, 1))), first, slices + 2, 1)
    norm = 1.0 / (ray_total * ((1.0 - share[:, 1:]) + share[:, :-1]))
    coef_now = (1.0 - share[:, 1:]) * norm
    coef_prev = share[:, :-1] * norm

    def by_block(coef):
        coef = coef[:, 1:].reshape(angles, blocks, BLOCK // HALF, HALF).transpose(1, 2, 0, 3)
        return jnp.broadcast_to(coef.reshape(blocks, BLOCK // HALF, angles * HALF, 1), (blocks, BLOCK // HALF, angles * HALF, LANES))

    def at_edge(coef):
        return jnp.broadcast_to(coef[:, :1], (angles, LANES))

    coefs = [by_block(c) for c in (coef_now, coef_prev, norm)]
    edge_coefs = [at_edge(c) for c in (coef_now, coef_prev, norm)]

    share_own = share[:, 1:-1]
    row_now = (first - bases)[:, None] + jnp.arange(slices, dtype=jnp.int32)[None, :]
    w_now = jnp.where((row_now >= 0) & (row_now < rows), 1.0 - share_own, 0.0)
    w_next = jnp.where((row_now + 1 >= 0) & (row_now + 1 < rows), share_own, 0.0)
    column_norm = jnp.einsum("ad,az->zd", weights, w_now + w_next, precision=lax.Precision.HIGHEST)
    scale = RELAX / column_norm

    eye = jnp.eye(HALF, dtype=jnp.float32)
    image_w = jnp.einsum("ad,yz->ayzd", weights, eye).reshape(angles * HALF, HALF * depth).astype(jnp.bfloat16)
    same = jnp.eye(BLOCK, dtype=jnp.float32)
    later = jnp.eye(BLOCK, k=-1, dtype=jnp.float32)
    pair = (
        w_next.T.reshape(blocks, BLOCK, 1, angles, 1) * same[None, :, None, None, :]
        + w_now.T.reshape(blocks, BLOCK, 1, angles, 1) * later[None, :, None, None, :]
    )
    spread_w = pair * weights.T[None, None, :, :, None] * scale.reshape(blocks, BLOCK, depth, 1, 1)
    spread_w = spread_w.reshape(blocks, BLOCK * depth, angles * BLOCK).astype(jnp.bfloat16)
    carry_w = (
        w_now.T.reshape(blocks, BLOCK, 1, angles)[:, 0] * weights.T[None] * scale.reshape(blocks, BLOCK, depth, 1)[:, 0]
    ).astype(jnp.bfloat16)
    return update(volume, left, right, seen, edge, coefs, edge_coefs, image_w, path_weights, spread_w, carry_w)


def solution(mesh):
    placed = (P(("groups", "slab"), None, None), P(("groups", "slab"), None, None), P(), P(), P())
    return jax.shard_map(
        on_device,
        mesh=mesh,
        in_specs=placed,
        out_specs=P(("groups", "slab"), None, None),
        check_vma=False,
    )
```

time: 912 us -> 251 us (0.28)
  waiting for transfers between devices: 572 us -> 135 us
  other arithmetic: 119 us -> 7.63 us
  local copies, waits for them, and re-layouts: 147 us -> 44.3 us
  matrix products: 46.5 us -> 0.2 us
  Pallas kernels: 0 us -> 36.2 us
  blocking collectives: 0 us -> 10.8 us
  loops' own time: 10.3 us -> 0 us
    all_to_all x1 -> x0, waiting for transfers between devices: 380 us -> none  [on_device(): lax.all_to_all(slots, 'slab', split_axis=0, concat_axis=0, tiled=True)]
    all_to_all x1, waiting for transfers between devices: 192 us -> 0.01 us  [on_device(): lax.all_to_all(outgoing, 'slab', split_axis=0, concat_axis=0, tiled=True)]
    ppermute x0 -> x2, waiting for transfers between devices: none -> 135 us  [the longest x1 135 us: on_device(): lax.ppermute(volume[:1], 'slab', [(i + 1, i) for i in range(nslab - 1)])]
    another operation x32 -> x2, other arithmetic: 90.9 us -> 0.03 us  [the longest x1 0.02 us: on_device(): jnp.tile(ends, (planes, 1, 1)).reshape(nslab * local, cols // LANES, LANES)]
    scatter x16 -> x0, local copies, waits for them, and re-layouts: 75.7 us -> none  [accumulate(): lax.dynamic_update_slice_in_dim(acc, current + parts[source], start, 0)]
    dot_general x3 -> x1, matrix products: 46.5 us -> 0.2 us  [on_device(): jnp.einsum('ad,az->zd', weights, w_now + w_next, precision=lax.Precision....]
    pallas_call x0 -> x1, Pallas kernels: none -> 36.2 us  [update(): pl.pallas_call(update_kernel, grid=(cols // width, blocks), in_specs=[pl....]
    gather x49 -> x0, local copies, waits for them, and re-layouts: 35.2 us -> none
  transfers between devices with their start and end apart: 2 -> 3, of which waited for: 2 -> 1; matrix products, arithmetic and copies ran while one was open for 0% -> 17% of each run, Pallas kernels for 0% -> 0%
where the time goes in v1:
time: 251 us; the launch traced here: 249 us
  waiting for transfers between devices  135 us (54%)
  local copies, waits for them, and re-layouts  44.3 us (18%)
  Pallas kernels  36.2 us (14%)
  starting transfers between devices  13.8 us (5%)
  blocking collectives  10.8 us (4%)
  other arithmetic  7.63 us (3%)
    ppermute x1, waiting for transfers between devices, on_device(): lax.ppermute(volume[:1], 'slab', [(i + 1, i) for i in range(nslab - 1)])  135 us
    pallas_call x1, Pallas kernels, update(): pl.pallas_call(update_kernel, grid=(cols // width, blocks), in_specs=[pl....  36.2 us
    mul x7, local copies, waits for them, and re-layouts, on_device(): pair * weights.T[None, None, :, :, None]  28.6 us
    all_to_all x1, blocking collectives, on_device(): lax.all_to_all(ends, 'slab', split_axis=0, concat_axis=0, tiled=True)  10.8 us
    all_to_all x1, starting transfers between devices, on_device(): lax.all_to_all(outgoing, 'slab', split_axis=0, concat_axis=0, tiled=True)  7.39 us
  transfers between devices with their start and end apart: 3, of which 1 were waited for; matrix products, arithmetic and copies ran while one was open for 17% of the time, Pallas kernels for 0%

profile of v1, /device:TPU:15, one launch (start us, length us, event | category | flops | bytes accessed | tf_op | source)
XLA Modules:
  0.0 249.2 jit_solution(1705960531916505896)
XLA Ops:
  0.0 1.2 dynamic_slice.6
  1.9 3.5 %fusion = bf16[1,512,2048]{2,1,0:T(8,128)(2,1)S(1)} fusion(s32[]{:T(128)} %bitcast, bf16[1,512,2048]{2,1,0:T(8,128)(2,1)} %param.6), kind=kLoop, calls=%fused_computation.3 | loop fusion | flops 4194304 | bytes 4194308 | tf_op jit(solution)/shard_map/vmap(jit(_roll_dynamic))/concatenate | solution.py:125
  5.6 10.8 %all_to_all.10 = bf16[16,16,128]{2,1,0:T(8,128)(2,1)} all-to-all(bf16[16,16,128]{2,1,0:T(8,128)(2,1)S(1)} %tile.24), channel_id=1, replica_groups=mesh['groups'=2,'slab'=16] {'slab'}, dimensions={0} | all-to-all | bytes 131072 | tf_op jit(solution)/shard_map/all_to_all | solution.py:131
  16.4 4.3 %tile.20 = bf16[4,4,128,2048]{3,2,1,0:T(8,128)(2,1)} broadcast(bf16[4,128,2048]{2,1,0:T(8,128)(2,1)S(1)} %bitcast.68), dimensions={1,2,3} | broadcast | bytes 10485760 | tf_op jit(solution)/shard_map/tile | solution.py:127
  20.7 7.4 %all-to-all-start = ((bf16[16,128,2048]{2,1,0:T(8,128)(2,1)}), bf16[16,128,2048]{2,1,0:T(8,128)(2,1)}, u32[]{:S(2)}, u32[]{:S(2)}) async-start(bf16[16,128,2048]{2,1,0:T(8,128)(2,1)} %bitcast.65), calls=%async_computation | async-start | bytes 16777216 | tf_op jit(solution)/shard_map/all_to_all | solution.py:128
  28.1 1.7 fusion.17
  29.8 2.3 collective-permute-start.1
  32.0 4.2 %collective-permute-start = (bf16[1,32,2048]{2,1,0:T(8,128)(2,1)}, bf16[1,32,2048]{2,1,0:T(8,128)(2,1)S(1)}, u32[]{:S(2)}, u32[]{:S(2)}) collective-permute-start(bf16[1,32,2048]{2,1,0:T(8,128)(2,1)} %get-tuple-element.19), channel_id=1, source_target_pairs={{0,1},{1,2},{2,3},{3,4},{4,5},{5,6},{6,7},{7,8},{8,9},{9,10},{10,1... | collective-permute-start | bytes 393224 | tf_op jit(solution)/shard_map/ppermute | solution.py:132
  36.3 0.7 copy.44
  37.3 0.3 copy.30
  37.7 0.6 slice.99
  38.3 0.2 convolution_divide_fusion
  38.6 0.7 mul.132
  39.3 0.6 slice.100
  39.9 0.7 copy.38
  40.6 0.7 copy.37
  41.9 0.7 reshape.126
  42.7 0.7 reshape.124
  43.6 0.8 mul.129
  44.4 0.2 copy.39
  44.7 1.0 multiply_add_fusion
  45.7 8.4 %mul.126 = f32[8,16,32,16,16]{2,1,4,3,0:T(8,128)} broadcast(f32[8,16,16,16]{1,3,2,0:T(8,128)S(1)} %multiply_add_fusion), dimensions={0,1,3,4} | broadcast | bytes 4325376 | tf_op jit(solution)/shard_map/mul | solution.py:167
  54.1 12.9 %mul.127 = f32[8,512,256]{1,2,0:T(8,128)} reshape(f32[8,16,32,16,16]{2,1,4,3,0:T(8,128)} %mul.126) | data formatting | bytes 8388608 | tf_op jit(solution)/shard_map/mul | solution.py:167
  67.0 5.4 %copy.40 = f32[8,512,256]{2,1,0:T(8,128)} copy(f32[8,512,256]{1,2,0:T(8,128)} %mul.127) | data formatting | bytes 8388608 | tf_op jit(solution)/shard_map/mul | solution.py:167
  72.4 0.7 slice_bitcast_fusion.1
  73.2 2.6 %multiply_convert_fusion.spread_ref = bf16[8,512,256]{2,1,0:T(8,128)(2,1)S(1)} fusion(f32[8,512,256]{2,1,0:T(8,128)} %copy.40, f32[8,512]{1,0:T(8,128)S(1)} %copy-done.5, f32[512,256]{1,0:T(8,128)S(1)} %copy.39), kind=kLoop, calls=%fused_computation.2 | loop fusion | flops 3145728 | bytes 6832128 | tf_op jit(solution)/shard_map/convert_element_type | solution.py:168
  75.8 0.7 slice_bitcast_fusion.3
  76.5 135.2 %collective-permute-done.1.right_ref = bf16[1,32,2048]{2,1,0:T(8,128)(2,1)S(1)} collective-permute-done((bf16[1,32,2048]{2,1,0:T(8,128)(2,1)}, bf16[1,32,2048]{2,1,0:T(8,128)(2,1)S(1)}, u32[]{:S(2)}, u32[]{:S(2)}) %collective-permute-start.1) | collective-permute-done | bytes 131104 | tf_op jit(solution)/shard_map/ppermute | solution.py:133
  212.0 0.3 broadcast_in_dim.60.now_ref
  212.3 0.3 broadcast_in_dim.64.inv_ref
  212.6 0.3 broadcast_in_dim.62.prev_ref
  213.0 36.2 %slab_update.1 = f32[128,32,2048]{2,1,0:T(8,128)} custom-call(bf16[128,32,2048]{2,1,0:T(8,128)(2,1)} %next_ref.1, bf16[128,32,2048]{2,1,0:T(8,128)(2,1)} %next_ref.1, bf16[1,32,2048]{2,1,0:T(8,128)(2,1)S(1)} %collective-permute-done.left_ref, bf16[1,32,2048]{2,1,0:T(8,128)(2,1)S(1)} %collective-permute-done.1.right_ref, ...), custom_call_target="tpu_custom_call" | custom-call | flops 536870912 | bytes 58720256 | tf_op jit(solution)/shard_map/slab_update/pallas_call | solution.py:81
  (57 shorter events, 1.7 us)
Async XLA Ops:
  20.7 15.6 %copy-start = (bf16[16,32]{1,0:T(8,128)(2,1)S(1)}, bf16[16,32]{1,0:T(8,128)(2,1)}, u32[]{:S(2)}) copy-start(bf16[16,32]{1,0:T(8,128)(2,1)} %weight_ref.1) | copy-start | bytes 3076
  20.7 16.6 %copy-start.4 = (f32[16,2048]{1,0:T(8,128)S(1)}, f32[16,2048]{1,0:T(8,128)}, u32[]{:S(2)}) copy-start(f32[16,2048]{1,0:T(8,128)} %param.8) | copy-start | bytes 393220
  20.7 16.9 %copy-start.11 = (s32[16]{0:T(128)S(1)}, s32[16]{0:T(128)}, u32[]{:S(2)}) copy-start(s32[16]{0:T(128)} %param.9) | copy-start | bytes 196
  20.7 191.1 %all-to-all-start = ((bf16[16,128,2048]{2,1,0:T(8,128)(2,1)}), bf16[16,128,2048]{2,1,0:T(8,128)(2,1)}, u32[]{:S(2)}, u32[]{:S(2)}) async-start(bf16[16,128,2048]{2,1,0:T(8,128)(2,1)} %bitcast.65), calls=%async_computation | async-start | bytes 16777216 | tf_op jit(solution)/shard_map/all_to_all | solution.py:128
  29.8 182.0 %collective-permute-start.1 = (bf16[1,32,2048]{2,1,0:T(8,128)(2,1)}, bf16[1,32,2048]{2,1,0:T(8,128)(2,1)S(1)}, u32[]{:S(2)}, u32[]{:S(2)}) collective-permute-start(bf16[1,32,2048]{2,1,0:T(8,128)(2,1)} %get-tuple-element.18), channel_id=1, source_target_pairs={{1,0},{2,1},{3,2},{4,3},{5,4},{6,5},{7,6},{8,7},{9,8},{10,9},{11,1... | collective-permute-start | bytes 393224 | tf_op jit(solution)/shard_map/ppermute | solution.py:133
  32.0 179.7 %collective-permute-start = (bf16[1,32,2048]{2,1,0:T(8,128)(2,1)}, bf16[1,32,2048]{2,1,0:T(8,128)(2,1)S(1)}, u32[]{:S(2)}, u32[]{:S(2)}) collective-permute-start(bf16[1,32,2048]{2,1,0:T(8,128)(2,1)} %get-tuple-element.19), channel_id=1, source_target_pairs={{0,1},{1,2},{2,3},{3,4},{4,5},{5,6},{6,7},{7,8},{8,9},{9,10},{10,1... | collective-permute-start | bytes 393224 | tf_op jit(solution)/shard_map/ppermute | solution.py:132
  41.5 1.2 copy-start.1
  41.5 1.2 copy-start.2
  67.0 6.1 %copy-start.6 = (f32[32,16]{1,0:T(8,128)S(1)}, f32[32,16]{1,0:T(8,128)}, u32[]{:S(2)}) copy-start(f32[32,16]{1,0:T(8,128)} %copy.44) | copy-start | bytes 6148
  67.0 6.1 %copy-start.9 = (f32[8,1,1,16]{3,1,0,2:T(1,128)S(1)}, f32[8,1,1,16]{3,1,0,2:T(1,128)}, u32[]{:S(2)}) copy-start(f32[8,1,1,16]{3,1,0,2:T(1,128)} %slice.99) | copy-start | bytes 1540
  67.0 6.1 %copy-start.10 = (f32[8,1,32,1]{2,1,0,3:T(1,128)S(1)}, f32[8,1,32,1]{2,1,0,3:T(1,128)}, u32[]{:S(2)}) copy-start(f32[8,1,32,1]{2,1,0,3:T(1,128)} %slice.100) | copy-start | bytes 3076
  67.0 6.2 %copy-start.5 = (f32[8,512]{1,0:T(8,128)S(1)}, f32[8,512]{1,0:T(8,128)}, u32[]{:S(2)}) copy-start(f32[8,512]{1,0:T(8,128)} %mul.132) | copy-start | bytes 49156
  72.4 4.1 %copy-start.3 = (bf16[16,16,128]{2,1,0:T(8,128)(2,1)S(1)}, bf16[16,16,128]{2,1,0:T(8,128)(2,1)}, u32[]{:S(2)}) copy-start(bf16[16,16,128]{2,1,0:T(8,128)(2,1)} %all_to_all.10) | copy-start | bytes 196612
  72.4 139.6 %copy-start.8 = (f32[8,2,128]{2,1,0:T(2,128)S(1)}, f32[8,2,128]{2,1,0:T(2,128)}, u32[]{:S(2)}) copy-start(f32[8,2,128]{2,1,0:T(2,128)} %reshape.124) | copy-start | bytes 24580
  72.4 139.9 %copy-start.7 = (f32[8,2,128]{2,1,0:T(2,128)S(1)}, f32[8,2,128]{2,1,0:T(2,128)}, u32[]{:S(2)}) copy-start(f32[8,2,128]{2,1,0:T(2,128)} %reshape.126) | copy-start | bytes 24580
